TPU v7x, 32 devices: a whole 2x2x4 slice. The times are simulated.
32 devices in a mesh: gx: 4 (over x, core), gz: 8 (over z, y).
Axes of the slice: x: 2, y: 2, z: 4, core: 2. Of those that a mesh axis runs over, the one named last changes fastest.
Arguments:
- source_field: float32 [8, 512, 4096], P('gz', None, 'gx'), may hold values from -8 to 8
- coupling: float32 [8], replicated, may hold values from 0.5 to 2
- spacing: float32 [8], replicated, may hold values from 0.5 to 2
Outputs:
- pressure: float32 [8, 512, 4096], P('gz', None, 'gx')
All inputs are finite; a program needn't handle non-finite values.
Results may differ from a plain program's by a relative error of at most 0.0003.
Values sent between devices are 32-bit elements; how exact they have to be, the bound alone decides.
A program may use at most 128 MiB of HBM per device.

v0:
```python
import functools
import math

import jax
import jax.numpy as jnp
import ml_dtypes
import numpy as np
from jax import lax
from jax.experimental import pallas as pl
from jax.experimental.pallas import tpu as pltpu
from jax.sharding import PartitionSpec as P

LANES = 128
MESH = pl.DeviceIdType.MESH


def cos_sin(product, period):
    angles = (product % period).astype(np.float64) * (2.0 * math.pi / period)
    return np.cos(angles), np.sin(angles)


def split_table(table):
    high = table.astype(np.float32).astype(ml_dtypes.bfloat16)
    low = (table - high.astype(np.float64)).astype(np.float32).astype(ml_dtypes.bfloat16)
    return high, low


def make_tables(span, stream, rows):
    outer = stream // LANES
    slots = outer // 2
    ks = np.arange(span)
    cosine, sine = cos_sin(ks[:, None] * ks[None, :], span)
    span_high, span_low = split_table(cosine + sine)
    lane = np.arange(LANES)
    cosine, sine = cos_sin(lane[:, None] * lane[None, :], LANES)
    regular = np.block([[cosine, -sine], [sine, cosine]])
    half_cos, half_sin = cos_sin(lane[:, None] * (slots + outer * lane[None, :]), stream)
    zeros = np.zeros((LANES, LANES))
    special = np.block([[cosine + sine, zeros], [zeros, half_cos + half_sin]])
    forward = np.stack([special, regular])
    inverse = np.stack([special.T, regular.T]) / (span * stream)
    forward_high, forward_low = split_table(forward)
    inverse_high, inverse_low = split_table(inverse)
    turn_cos, turn_sin = cos_sin(np.arange(slots)[:, None] * lane[None, :], stream)
    wave = np.arange(slots)[:, None] + outer * np.concatenate([lane, lane])[None, :]
    wave[0, LANES:] += slots
    eigen_stream = 2.0 - 2.0 * cos_sin(wave, stream)[0]
    eigen_stream = np.ascontiguousarray(np.broadcast_to(eigen_stream[:, None, :], (slots, rows, 2 * LANES)))
    eigen_span = 2.0 - 2.0 * cos_sin(ks, span)[0]
    eigen_span = np.broadcast_to(eigen_span[:, None], (span, 2 * LANES)).reshape(span // rows, rows, 2 * LANES)
    return (
        span_high, span_low, forward_high, forward_low, inverse_high, inverse_low,
        turn_cos.astype(np.float32), turn_sin.astype(np.float32),
        eigen_stream.astype(np.float32), np.ascontiguousarray(eigen_span).astype(np.float32),
    )


def real_transform(values):
    count = len(values)
    if count == 2:
        return [(values[0] + values[1], None), (values[0] - values[1], None)]
    even = real_transform(values[0::2])
    odd = real_transform(values[1::2])
    result = [None] * (count // 2 + 1)
    quarter = count // 4
    result[0] = (even[0][0] + odd[0][0], None)
    result[count // 2] = (even[0][0] - odd[0][0], None)
    result[quarter] = (even[quarter][0], -odd[quarter][0])
    for k in range(1, quarter):
        angle = 2.0 * math.pi * k / count
        cosine, sine = math.cos(angle), math.sin(angle)
        odd_real, odd_imag = odd[k]
        turned_real = odd_real * cosine + odd_imag * sine
        turned_imag = odd_imag * cosine - odd_real * sine
        even_real, even_imag = even[k]
        result[k] = (even_real + turned_real, even_imag + turned_imag)
        result[count // 2 - k] = (even_real - turned_real, turned_imag - even_imag)
    return result


def real_inverse(pairs):
    count = 2 * (len(pairs) - 1)
    if count == 2:
        return [pairs[0][0] + pairs[1][0], pairs[0][0] - pairs[1][0]]
    quarter = count // 4
    even, odd = [None] * (quarter + 1), [None] * (quarter + 1)
    even[0] = (pairs[0][0] + pairs[count // 2][0], None)
    odd[0] = (pairs[0][0] - pairs[count // 2][0], None)
    even[quarter] = (2.0 * pairs[quarter][0], None)
    odd[quarter] = (-2.0 * pairs[quarter][1], None)
    for k in range(1, quarter):
        angle = 2.0 * math.pi * k / count
        cosine, sine = math.cos(angle), math.sin(angle)
        low_real, low_imag = pairs[k]
        high_real, high_imag = pairs[count // 2 - k]
        even[k] = (low_real + high_real, low_imag - high_imag)
        diff_real, diff_imag = low_real - high_real, low_imag + high_imag
        odd[k] = (diff_real * cosine - diff_imag * sine, diff_imag * cosine + diff_real * sine)
    even_values, odd_values = real_inverse(even), real_inverse(odd)
    return [(even_values if n % 2 == 0 else odd_values)[n // 2] for n in range(count)]


def split_value(value):
    high = value.astype(jnp.bfloat16)
    return high, (value - high.astype(jnp.float32)).astype(jnp.bfloat16)


def dot3(left, right):
    dot = functools.partial(jnp.dot, preferred_element_type=jnp.float32)
    return dot(left[0], right[0]) + (dot(left[0], right[1]) + dot(left[1], right[0]))


def kernel(
    cfg, coupling, spacing, field, span_high, span_low, fwd_high, fwd_low, inv_high, inv_low,
    turn_cos, turn_sin, eig_stream, eig_span, out,
    field_high, field_low, send_box, columns, staging, spectrum, pivots_low, pivots_high, middle,
    reduced, edge_down, from_below, from_above, solved, returned,
    go_send, go_recv, up_send, up_recv, down_send, down_recv, back_send, back_recv,
):
    gx_count, group, planes, chunks, rows, levels = cfg
    peers = gx_count * group
    blocks = field.shape[2] // LANES
    outer = blocks * gx_count
    slots = outer // 2
    level_count = levels * planes
    gx = lax.axis_index("gx")
    gz = lax.axis_index("gz")
    plane = gz // group
    row = gz % group
    me = gx * group + row
    first = plane * levels

    def partner(step):
        step_gx, step_row = step // group, step % group
        to_gx, to_row = (gx + step_gx) % gx_count, (row + step_row) % group
        from_gx, from_row = (gx + gx_count - step_gx) % gx_count, (row + group - step_row) % group
        return (to_gx, to_row), (from_gx, from_row)

    barrier = pltpu.get_barrier_semaphore()
    for step in range(1, peers):
        (to_gx, to_row), _ = partner(step)
        pl.semaphore_signal(barrier, inc=1, device_id=(to_gx, plane * group + to_row), device_id_type=MESH)

    @pl.when(plane > 0)
    def _():
        pl.semaphore_signal(barrier, inc=1, device_id=(gx, gz - group), device_id_type=MESH)

    @pl.when(plane < planes - 1)
    def _():
        pl.semaphore_signal(barrier, inc=1, device_id=(gx, gz + group), device_id_type=MESH)

    def go_copy(chunk, step):
        (to_gx, to_row), _ = partner(step)
        return pltpu.make_async_remote_copy(
            src_ref=send_box.at[chunk, to_gx * group + to_row],
            dst_ref=columns.at[chunk, row, pl.ds(gx * blocks, blocks)],
            send_sem=go_send.at[chunk, step], recv_sem=go_recv.at[chunk, step],
            device_id=(to_gx, plane * group + to_row), device_id_type=MESH)

    def go_arrival(chunk, step):
        _, (from_gx, from_row) = partner(step)
        return pltpu.make_async_remote_copy(
            src_ref=send_box.at[chunk, 0],
            dst_ref=columns.at[chunk, from_row, pl.ds(from_gx * blocks, blocks)],
            send_sem=go_send.at[chunk, step], recv_sem=go_recv.at[chunk, step],
            device_id=(from_gx, plane * group + from_row), device_id_type=MESH)

    def back_copy(chunk, step):
        (to_gx, to_row), _ = partner(step)
        return pltpu.make_async_remote_copy(
            src_ref=solved.at[chunk, to_row, pl.ds(to_gx * blocks, blocks)],
            dst_ref=returned.at[chunk, me],
            send_sem=back_send.at[chunk, step], recv_sem=back_recv.at[chunk, step],
            device_id=(to_gx, plane * group + to_row), device_id_type=MESH)

    def back_arrival(chunk, step):
        _, (from_gx, from_row) = partner(step)
        return pltpu.make_async_remote_copy(
            src_ref=solved.at[chunk, 0, pl.ds(0, blocks)],
            dst_ref=returned.at[chunk, from_gx * group + from_row],
            send_sem=back_send.at[chunk, step], recv_sem=back_recv.at[chunk, step],
            device_id=(from_gx, plane * group + from_row), device_id_type=MESH)

    def up_copy(chunk):
        return pltpu.make_async_remote_copy(
            src_ref=reduced.at[chunk, levels - 1], dst_ref=from_below.at[chunk],
            send_sem=up_send.at[chunk], recv_sem=up_recv.at[chunk],
            device_id=(gx, (gz + group) % (planes * group)), device_id_type=MESH)

    def down_copy(chunk):
        return pltpu.make_async_remote_copy(
            src_ref=edge_down.at[chunk], dst_ref=from_above.at[chunk],
            send_sem=down_send.at[chunk], recv_sem=down_recv.at[chunk],
            device_id=(gx, (gz + planes * group - group) % (planes * group)), device_id_type=MESH)

    def below(level):
        return coupling[level]

    def above(level):
        return jnp.where(level + 1 < level_count, coupling[jnp.minimum(level + 1, level_count - 1)], 0.0)

    field_high[...], field_low[...] = split_value(field[0])

    def span_step(chunk, carry):
        take = pl.ds(pl.multiple_of(chunk * (peers * rows), peers * rows), peers * rows)
        left = (span_high[take, :], span_low[take, :])
        width = min(2, blocks)
        for block in range(0, blocks, width):
            cols = slice(block * LANES, (block + width) * LANES)
            modes = dot3(left, (field_high[:, cols], field_low[:, cols]))
            for part in range(width):
                piece = modes[:, part * LANES:(part + 1) * LANES]
                send_box[chunk, :, block + part] = piece.reshape(peers, rows, LANES)

        @pl.when(chunk == 0)
        def _():
            expected = peers - 1 + jnp.where(plane > 0, 1, 0) + jnp.where(plane < planes - 1, 1, 0)
            pl.semaphore_wait(barrier, expected)

        for step in range(1, peers):
            go_copy(chunk, step).start()
        columns[chunk, row, pl.ds(gx * blocks, blocks)] = send_box[chunk, me]
        return carry

    lax.fori_loop(0, chunks, span_step, 0)

    part_slots = min(4, slots)
    parts = slots // part_slots

    def coefficients(chunk):
        def part_step(part, carry):
            take = pl.ds(part * part_slots, part_slots)
            lam = eig_span[chunk * peers + me][None] + eig_stream[take]

            def from_ground(level, ratio):
                pivot = lam * spacing[level] + below(level) + above(level) - below(level) * ratio
                return above(level) / pivot

            ratio = lax.fori_loop(0, first, from_ground, jnp.zeros_like(lam))
            for own in range(levels):
                level = first + own
                pivot = lam * spacing[level] + below(level) + above(level) - below(level) * ratio
                factor = 1.0 / pivot
                pivots_low[chunk, own, take] = factor
                ratio = above(level) * factor

            def from_top(count, ratio_top):
                level = level_count - 1 - count
                pivot = lam * spacing[level] + below(level) + above(level) - above(level) * ratio_top
                return below(level) / pivot

            ratio_top = lax.fori_loop(0, level_count - first - levels, from_top, jnp.zeros_like(lam))
            middle[chunk, take] = 1.0 / (1.0 - ratio * ratio_top)
            for own in reversed(range(levels)):
                level = first + own
                pivot = lam * spacing[level] + below(level) + above(level) - above(level) * ratio_top
                factor = 1.0 / pivot
                pivots_high[chunk, own, take] = factor
                ratio_top = below(level) * factor
            return carry

        lax.fori_loop(0, parts, part_step, 0)

    tiles = rows // 8

    def stream_forward(chunk):
        def tile_step(index, carry):
            own, tile = index // tiles, index % tiles
            inner = pl.ds(pl.multiple_of(tile * 8, 8), 8)
            place = pl.ds(pl.multiple_of(own * rows + tile * 8, 8), 8)
            pairs = real_transform([columns[chunk, own, n, inner, :] for n in range(outer)])
            staging[0, place, :LANES] = pairs[0][0]
            staging[0, place, LANES:] = pairs[slots][0]
            for k in range(1, slots):
                real, imag = pairs[k]
                cosine, sine = turn_cos[k:k + 1, :], turn_sin[k:k + 1, :]
                staging[k, place, :LANES] = real * cosine + imag * sine
                staging[k, place, LANES:] = imag * cosine - real * sine
            return carry

        lax.fori_loop(0, levels * tiles, tile_step, 0)
        special = dot3(split_value(staging[0]), (fwd_high[0], fwd_low[0]))
        spectrum[chunk, 0] = special.reshape(levels, rows, 2 * LANES)
        rest = staging[1:].reshape((slots - 1) * levels * rows, 2 * LANES)
        regular = dot3(split_value(rest), (fwd_high[1], fwd_low[1]))
        spectrum[chunk, 1:] = regular.reshape(slots - 1, levels, rows, 2 * LANES)

    def sweep_up(chunk):
        @pl.when(plane > 0)
        def _():
            up_copy(chunk).wait_recv()

        @pl.when(plane == 0)
        def _():
            from_below[chunk] = jnp.zeros(from_below.shape[1:], jnp.float32)

        def part_step(part, carry):
            take = pl.ds(part * part_slots, part_slots)
            value = from_below[chunk, take]
            for own in range(levels):
                level = first + own
                value = (spacing[level] * spectrum[chunk, take, own] + below(level) * value) * pivots_low[chunk, own, take]
                reduced[chunk, own, take] = value
            return carry

        lax.fori_loop(0, parts, part_step, 0)

        @pl.when(plane < planes - 1)
        def _():
            up_copy(chunk).start()

    def sweep_down(chunk):
        @pl.when(plane < planes - 1)
        def _():
            down_copy(chunk).wait_recv()

        @pl.when(plane == planes - 1)
        def _():
            from_above[chunk] = jnp.zeros(from_above.shape[1:], jnp.float32)

        @pl.when(plane > 0)
        def _():
            def part_step(part, carry):
                take = pl.ds(part * part_slots, part_slots)
                value = from_above[chunk, take]
                for own in reversed(range(levels)):
                    level = first + own
                    value = (spacing[level] * spectrum[chunk, take, own] + above(level) * value) * pivots_high[chunk, own, take]
                edge_down[chunk, take] = value
                return carry

            lax.fori_loop(0, parts, part_step, 0)
            down_copy(chunk).start()

    def finish(chunk):
        def part_step(part, carry):
            take = pl.ds(part * part_slots, part_slots)
            value = from_above[chunk, take]
            for own in reversed(range(levels)):
                value = reduced[chunk, own, take] + above(first + own) * pivots_low[chunk, own, take] * value
                if own == levels - 1:
                    value = value * middle[chunk, take]
                staging[take, own * rows:(own + 1) * rows, :] = value
            return carry

        lax.fori_loop(0, parts, part_step, 0)
        special = dot3(split_value(staging[0]), (inv_high[0], inv_low[0]))
        rest = staging[1:].reshape((slots - 1) * levels * rows, 2 * LANES)
        regular = dot3(split_value(rest), (inv_high[1], inv_low[1]))
        staging[0] = special
        staging[1:] = regular.reshape(slots - 1, levels * rows, 2 * LANES)

        def tile_step(index, carry):
            own, tile = index // tiles, index % tiles
            inner = pl.ds(pl.multiple_of(tile * 8, 8), 8)
            place = pl.ds(pl.multiple_of(own * rows + tile * 8, 8), 8)
            pairs = [(staging[0, place, :LANES], None)]
            for k in range(1, slots):
                real, imag = staging[k, place, :LANES], staging[k, place, LANES:]
                cosine, sine = turn_cos[k:k + 1, :], turn_sin[k:k + 1, :]
                pairs.append((real * cosine - imag * sine, real * sine + imag * cosine))
            pairs.append((staging[0, place, LANES:], None))
            for n, value in enumerate(real_inverse(pairs)):
                solved[chunk, own, n, inner, :] = value
            return carry

        lax.fori_loop(0, levels * tiles, tile_step, 0)
        for step in range(1, peers):
            back_copy(chunk, step).start()
        returned[chunk, me] = solved[chunk, row, pl.ds(gx * blocks, blocks)]

    lag_down = planes - 1 - plane
    lag = jnp.maximum(plane, lag_down)

    def step(now, carry):
        @pl.when(now < chunks)
        def _():
            coefficients(now)
            for peer in range(1, peers):
                go_arrival(now, peer).wait_recv()
            stream_forward(now)

        @pl.when(jnp.logical_and(now >= plane, now < plane + chunks))
        def _():
            sweep_up(now - plane)

        @pl.when(jnp.logical_and(now >= lag_down, now < lag_down + chunks))
        def _():
            sweep_down(now - lag_down)

        @pl.when(jnp.logical_and(now >= lag, now < lag + chunks))
        def _():
            finish(now - lag)

        return carry

    lax.fori_loop(0, chunks + planes - 1, step, 0)

    def arrive(chunk, carry):
        for peer in range(1, peers):
            back_arrival(chunk, peer).wait_recv()
        return carry

    lax.fori_loop(0, chunks, arrive, 0)
    span = field.shape[1]
    width = min(2, blocks)
    for block in range(0, blocks, width):
        pieces = [returned[:, :, block + part].reshape(span, LANES) for part in range(width)]
        right = split_value(jnp.concatenate(pieces, axis=1) if width > 1 else pieces[0])
        out[0, :, block * LANES:(block + width) * LANES] = dot3((span_high[...], span_low[...]), right)

    def drain(chunk, carry):
        for peer in range(1, peers):
            go_copy(chunk, peer).wait_send()
            back_copy(chunk, peer).wait_send()

        @pl.when(plane < planes - 1)
        def _():
            up_copy(chunk).wait_send()

        @pl.when(plane > 0)
        def _():
            down_copy(chunk).wait_send()

        return carry

    lax.fori_loop(0, chunks, drain, 0)


def local(mesh_shape, source_field, coupling, spacing):
    gx_count, gz_count = mesh_shape["gx"], mesh_shape["gz"]
    own, span, part = source_field.shape
    assert own == 1
    group = gz_count // 4 if gz_count % 4 == 0 else 1
    planes = gz_count // group
    levels = group
    peers = gx_count * group
    stream = part * gx_count
    share = span // peers
    chunks = 4
    while share % (8 * chunks):
        chunks //= 2
    rows = share // chunks
    blocks = part // LANES
    outer = stream // LANES
    slots = outer // 2
    tables = make_tables(span, stream, rows)
    f32 = jnp.float32
    wide = (slots, rows, 2 * LANES)
    dma = pltpu.SemaphoreType.DMA
    vmem = pl.BlockSpec(memory_space=pltpu.VMEM)
    smem = pl.BlockSpec(memory_space=pltpu.SMEM)
    cfg = (gx_count, group, planes, chunks, rows, levels)
    return pl.pallas_call(
        functools.partial(kernel, cfg),
        out_shape=jax.ShapeDtypeStruct(source_field.shape, f32),
        in_specs=[smem, smem] + [vmem] * 11,
        out_specs=vmem,
        scratch_shapes=[
            pltpu.VMEM((span, part), jnp.bfloat16),
            pltpu.VMEM((span, part), jnp.bfloat16),
            pltpu.VMEM((chunks, peers, blocks, rows, LANES), f32),
            pltpu.VMEM((chunks, levels, outer, rows, LANES), f32),
            pltpu.VMEM((slots, levels * rows, 2 * LANES), f32),
            pltpu.VMEM((chunks, slots, levels, rows, 2 * LANES), f32),
            pltpu.VMEM((chunks, levels) + wide, f32),
            pltpu.VMEM((chunks, levels) + wide, f32),
            pltpu.VMEM((chunks,) + wide, f32),
            pltpu.VMEM((chunks, levels) + wide, f32),
            pltpu.VMEM((chunks,) + wide, f32),
            pltpu.VMEM((chunks,) + wide, f32),
            pltpu.VMEM((chunks,) + wide, f32),
            pltpu.VMEM((chunks, levels, outer, rows, LANES), f32),
            pltpu.VMEM((chunks, peers, blocks, rows, LANES), f32),
            dma((chunks, peers)), dma((chunks, peers)),
            dma((chunks,)), dma((chunks,)), dma((chunks,)), dma((chunks,)),
            dma((chunks, peers)), dma((chunks, peers)),
        ],
        compiler_params=pltpu.CompilerParams(
            collective_id=0, has_side_effects=True, vmem_limit_bytes=56 * 1024 * 1024),
        cost_estimate=pl.CostEstimate(flops=8 * 10**9, bytes_accessed=8 * 2**20, transcendentals=0),
    )(coupling, spacing, source_field, *(jnp.asarray(table) for table in tables))


def solution(mesh):
    in_specs = (P("gz", None, "gx"), P(), P())
    out_specs = P("gz", None, "gx")
    return jax.shard_map(
        functools.partial(local, dict(mesh.shape)), mesh=mesh,
        in_specs=in_specs, out_specs=out_specs, check_vma=False)
```

profile of v0, /device:TPU:0, one launch (start us, length us, event | category | flops | bytes accessed | tf_op | source)
XLA Modules:
  0.0 70.7 jit_solution(17014672469619000449)
XLA Ops:
  0.0 67.6 %shard_map.127 = f32[1,512,1024]{2,1,0:T(8,128)} custom-call(f32[8]{0:T(128)} %coupling.1, f32[8]{0:T(128)} %spacing.1, f32[1,512,1024]{2,1,0:T(8,128)} %field.1, bf16[512,512]{1,0:T(8,128)(2,1)} %constant.20.clone.span_high, bf16[512,512]{1,0:T(8,128)(2,1)} %constant.21.clone.span_low, bf16[2,256,256]{2,1,0:T(8,128)(2,1)} %constant.22.clone.fwd_high, ...), custom_call_target="tpu_custom_call" | custom-call | flops 8000000000 | bytes 8388608 | tf_op jit(solution)/shard_map/pallas_call | solution.py:454
  67.6 3.2 %copy.15 = f32[1,512,1024]{2,1,0:T(8,128)} copy(f32[1,512,1024]{2,1,0:T(8,128)} %shard_map.127) | data formatting | bytes 4194304
where the time goes:
time: 71.6 us; the launch traced here: 70.7 us
  Pallas kernels  67.6 us (94%)
  local copies, waits for them, and re-layouts  3.16 us (4%)
    pallas_call x1, Pallas kernels, local(): pl.pallas_call(functools.partial(kernel, cfg), out_shape=jax.ShapeDtypeSt...  67.6 us
    unnamed x1, local copies, waits for them, and re-layouts  3.16 us

commit v1 on v0

--- a/solution.py
+++ b/solution.py
@@ -117,7 +117,7 @@
     reduced, edge_down, from_below, from_above, solved, returned,
     go_send, go_recv, up_send, up_recv, down_send, down_recv, back_send, back_recv,
 ):
-    gx_count, group, planes, chunks, rows, levels = cfg
+    gx_count, group, planes, chunks, rows, levels, batch = cfg
     peers = gx_count * group
     blocks = field.shape[2] // LANES
     outer = blocks * gx_count
@@ -201,8 +201,9 @@
 
     field_high[...], field_low[...] = split_value(field[0])
 
-    def span_step(chunk, carry):
-        take = pl.ds(pl.multiple_of(chunk * (peers * rows), peers * rows), peers * rows)
+    def span_step(turn, carry):
+        height = batch * peers * rows
+        take = pl.ds(pl.multiple_of(turn * height, height), height)
         left = (span_high[take, :], span_low[take, :])
         width = min(2, blocks)
         for block in range(0, blocks, width):
@@ -210,21 +211,24 @@
             modes = dot3(left, (field_high[:, cols], field_low[:, cols]))
             for part in range(width):
                 piece = modes[:, part * LANES:(part + 1) * LANES]
-                send_box[chunk, :, block + part] = piece.reshape(peers, rows, LANES)
-
-        @pl.when(chunk == 0)
+                piece = piece.reshape(batch, peers, rows, LANES)
+                send_box[pl.ds(turn * batch, batch), :, block + part] = piece
+
+        @pl.when(turn == 0)
         def _():
             expected = peers - 1 + jnp.where(plane > 0, 1, 0) + jnp.where(plane < planes - 1, 1, 0)
             pl.semaphore_wait(barrier, expected)
 
-        for step in range(1, peers):
-            go_copy(chunk, step).start()
-        columns[chunk, row, pl.ds(gx * blocks, blocks)] = send_box[chunk, me]
+        for index in range(batch):
+            chunk = turn * batch + index
+            for step in range(1, peers):
+                go_copy(chunk, step).start()
+            columns[chunk, row, pl.ds(gx * blocks, blocks)] = send_box[chunk, me]
         return carry
 
-    lax.fori_loop(0, chunks, span_step, 0)
-
-    part_slots = min(4, slots)
+    lax.fori_loop(0, chunks // batch, span_step, 0)
+
+    part_slots = min(max(1, 64 // rows), slots)
     parts = slots // part_slots
 
     def coefficients(chunk):
@@ -401,13 +405,21 @@
             back_arrival(chunk, peer).wait_recv()
         return carry
 
-    lax.fori_loop(0, chunks, arrive, 0)
     span = field.shape[1]
     width = min(2, blocks)
-    for block in range(0, blocks, width):
-        pieces = [returned[:, :, block + part].reshape(span, LANES) for part in range(width)]
-        right = split_value(jnp.concatenate(pieces, axis=1) if width > 1 else pieces[0])
-        out[0, :, block * LANES:(block + width) * LANES] = dot3((span_high[...], span_low[...]), right)
+    halves = 2 if chunks % 2 == 0 else 1
+    depth = span // halves
+    for half in range(halves):
+        lax.fori_loop(half * (chunks // halves), (half + 1) * (chunks // halves), arrive, 0)
+        near = slice(half * depth, (half + 1) * depth)
+        here = slice(half * (chunks // halves), (half + 1) * (chunks // halves))
+        left = (span_high[:, near], span_low[:, near])
+        for block in range(0, blocks, width):
+            pieces = [returned[here, :, block + part].reshape(depth, LANES) for part in range(width)]
+            right = split_value(jnp.concatenate(pieces, axis=1) if width > 1 else pieces[0])
+            value = dot3(left, right)
+            cols = slice(block * LANES, (block + width) * LANES)
+            out[0, :, cols] = value if half == 0 else out[0, :, cols] + value
 
     def drain(chunk, carry):
         for peer in range(1, peers):
@@ -437,10 +449,11 @@
     peers = gx_count * group
     stream = part * gx_count
     share = span // peers
-    chunks = 4
+    chunks = 8
     while share % (8 * chunks):
         chunks //= 2
     rows = share // chunks
+    batch = 2 if chunks % 2 == 0 and peers * rows < 128 else 1
     blocks = part // LANES
     outer = stream // LANES
     slots = outer // 2
@@ -450,7 +463,7 @@
     dma = pltpu.SemaphoreType.DMA
     vmem = pl.BlockSpec(memory_space=pltpu.VMEM)
     smem = pl.BlockSpec(memory_space=pltpu.SMEM)
-    cfg = (gx_count, group, planes, chunks, rows, levels)
+    cfg = (gx_count, group, planes, chunks, rows, levels, batch)
     return pl.pallas_call(
         functools.partial(kernel, cfg),
         out_shape=jax.ShapeDtypeStruct(source_field.shape, f32),

time: 71.6 us -> 68.7 us (0.959)
  Pallas kernels: 67.6 us -> 65.3 us
    pallas_call x1, Pallas kernels: 67.6 us -> 65.3 us  [local(): pl.pallas_call(functools.partial(kernel, cfg), out_shape=jax.ShapeDtypeSt...]
where the time goes in v1:
time: 68.7 us; the launch traced here: 68.5 us
  Pallas kernels  65.3 us (95%)
  local copies, waits for them, and re-layouts  3.16 us (5%)
    pallas_call x1, Pallas kernels, local(): pl.pallas_call(functools.partial(kernel, cfg), out_shape=jax.ShapeDtypeSt...  65.3 us
    unnamed x1, local copies, waits for them, and re-layouts  3.16 us

profile of v1, /device:TPU:0, one launch (start us, length us, event | category | flops | bytes accessed | tf_op | source)
XLA Modules:
  0.0 68.5 jit_solution(6688343306465531111)
XLA Ops:
  0.0 65.3 %shard_map.127 = f32[1,512,1024]{2,1,0:T(8,128)} custom-call(f32[8]{0:T(128)} %coupling.1, f32[8]{0:T(128)} %spacing.1, f32[1,512,1024]{2,1,0:T(8,128)} %field.1, bf16[512,512]{1,0:T(8,128)(2,1)} %constant.20.clone.span_high, bf16[512,512]{1,0:T(8,128)(2,1)} %constant.21.clone.span_low, bf16[2,256,256]{2,1,0:T(8,128)(2,1)} %constant.22.clone.fwd_high, ...), custom_call_target="tpu_custom_call" | custom-call | flops 8000000000 | bytes 8388608 | tf_op jit(solution)/shard_map/pallas_call | solution.py:467
  65.3 3.2 %copy.15 = f32[1,512,1024]{2,1,0:T(8,128)} copy(f32[1,512,1024]{2,1,0:T(8,128)} %shard_map.127) | data formatting | bytes 4194304

commit v2 on v1

--- a/solution.py
+++ b/solution.py
@@ -106,8 +106,15 @@
 
 
 def dot3(left, right):
-    dot = functools.partial(jnp.dot, preferred_element_type=jnp.float32)
-    return dot(left[0], right[0]) + (dot(left[0], right[1]) + dot(left[1], right[0]))
+    wide = jnp.concatenate([left[0], left[1], left[0]], axis=1)
+    tall = jnp.concatenate([right[0], right[0], right[1]], axis=0)
+    return jnp.dot(wide, tall, preferred_element_type=jnp.float32)
+
+
+def inverse_of(value):
+    guess = pl.reciprocal(value, approx=True)
+    guess = guess * (2.0 - value * guess)
+    return guess * (2.0 - value * guess)
 
 
 def kernel(
@@ -131,14 +138,11 @@
     first = plane * levels
 
     def partner(step):
-        step_gx, step_row = step // group, step % group
-        to_gx, to_row = (gx + step_gx) % gx_count, (row + step_row) % group
-        from_gx, from_row = (gx + gx_count - step_gx) % gx_count, (row + group - step_row) % group
-        return (to_gx, to_row), (from_gx, from_row)
+        return (gx + step // group) % gx_count, (row + step % group) % group
 
     barrier = pltpu.get_barrier_semaphore()
     for step in range(1, peers):
-        (to_gx, to_row), _ = partner(step)
+        to_gx, to_row = partner(step)
         pl.semaphore_signal(barrier, inc=1, device_id=(to_gx, plane * group + to_row), device_id_type=MESH)
 
     @pl.when(plane > 0)
@@ -150,36 +154,24 @@
         pl.semaphore_signal(barrier, inc=1, device_id=(gx, gz + group), device_id_type=MESH)
 
     def go_copy(chunk, step):
-        (to_gx, to_row), _ = partner(step)
+        to_gx, to_row = partner(step)
         return pltpu.make_async_remote_copy(
             src_ref=send_box.at[chunk, to_gx * group + to_row],
             dst_ref=columns.at[chunk, row, pl.ds(gx * blocks, blocks)],
-            send_sem=go_send.at[chunk, step], recv_sem=go_recv.at[chunk, step],
+            send_sem=go_send.at[chunk], recv_sem=go_recv.at[chunk],
             device_id=(to_gx, plane * group + to_row), device_id_type=MESH)
 
-    def go_arrival(chunk, step):
-        _, (from_gx, from_row) = partner(step)
-        return pltpu.make_async_remote_copy(
-            src_ref=send_box.at[chunk, 0],
-            dst_ref=columns.at[chunk, from_row, pl.ds(from_gx * blocks, blocks)],
-            send_sem=go_send.at[chunk, step], recv_sem=go_recv.at[chunk, step],
-            device_id=(from_gx, plane * group + from_row), device_id_type=MESH)
+    def all_blocks(box, chunk, sem):
+        blocks_here = box.at[chunk, pl.ds(0, peers - 1)]
+        pltpu.make_async_copy(blocks_here, blocks_here, sem.at[chunk]).wait()
 
     def back_copy(chunk, step):
-        (to_gx, to_row), _ = partner(step)
+        to_gx, to_row = partner(step)
         return pltpu.make_async_remote_copy(
             src_ref=solved.at[chunk, to_row, pl.ds(to_gx * blocks, blocks)],
             dst_ref=returned.at[chunk, me],
-            send_sem=back_send.at[chunk, step], recv_sem=back_recv.at[chunk, step],
+            send_sem=back_send.at[chunk], recv_sem=back_recv.at[chunk],
             device_id=(to_gx, plane * group + to_row), device_id_type=MESH)
-
-    def back_arrival(chunk, step):
-        _, (from_gx, from_row) = partner(step)
-        return pltpu.make_async_remote_copy(
-            src_ref=solved.at[chunk, 0, pl.ds(0, blocks)],
-            dst_ref=returned.at[chunk, from_gx * group + from_row],
-            send_sem=back_send.at[chunk, step], recv_sem=back_recv.at[chunk, step],
-            device_id=(from_gx, plane * group + from_row), device_id_type=MESH)
 
     def up_copy(chunk):
         return pltpu.make_async_remote_copy(
@@ -236,31 +228,33 @@
             take = pl.ds(part * part_slots, part_slots)
             lam = eig_span[chunk * peers + me][None] + eig_stream[take]
 
-            def from_ground(level, ratio):
-                pivot = lam * spacing[level] + below(level) + above(level) - below(level) * ratio
-                return above(level) / pivot
-
-            ratio = lax.fori_loop(0, first, from_ground, jnp.zeros_like(lam))
+            def diagonal(level):
+                return lam * spacing[level] + (below(level) + above(level))
+
+            def from_ground(level, pair):
+                now, before = pair
+                return diagonal(level) * now - (below(level) * below(level)) * before, now
+
+            def from_top(count, pair):
+                level = level_count - 1 - count
+                now, before = pair
+                return diagonal(level) * now - (above(level) * above(level)) * before, now
+
+            nought = lam * 0.0
+            start = (nought + 1.0, nought)
+            low = lax.fori_loop(0, first, from_ground, start)
             for own in range(levels):
-                level = first + own
-                pivot = lam * spacing[level] + below(level) + above(level) - below(level) * ratio
-                factor = 1.0 / pivot
-                pivots_low[chunk, own, take] = factor
-                ratio = above(level) * factor
-
-            def from_top(count, ratio_top):
-                level = level_count - 1 - count
-                pivot = lam * spacing[level] + below(level) + above(level) - above(level) * ratio_top
-                return below(level) / pivot
-
-            ratio_top = lax.fori_loop(0, level_count - first - levels, from_top, jnp.zeros_like(lam))
-            middle[chunk, take] = 1.0 / (1.0 - ratio * ratio_top)
+                after = from_ground(first + own, low)
+                pivots_low[chunk, own, take] = low[0] * inverse_of(after[0])
+                low = after
+            top = lax.fori_loop(0, level_count - first - levels, from_top, start)
+            edge = above(first + levels - 1)
+            both = low[0] * top[0]
+            middle[chunk, take] = both * inverse_of(both - (edge * edge) * (low[1] * top[1]))
             for own in reversed(range(levels)):
-                level = first + own
-                pivot = lam * spacing[level] + below(level) + above(level) - above(level) * ratio_top
-                factor = 1.0 / pivot
-                pivots_high[chunk, own, take] = factor
-                ratio_top = below(level) * factor
+                after = from_top(level_count - 1 - first - own, top)
+                pivots_high[chunk, own, take] = top[0] * inverse_of(after[0])
+                top = after
             return carry
 
         lax.fori_loop(0, parts, part_step, 0)
@@ -380,8 +374,7 @@
         @pl.when(now < chunks)
         def _():
             coefficients(now)
-            for peer in range(1, peers):
-                go_arrival(now, peer).wait_recv()
+            all_blocks(send_box, now, go_recv)
             stream_forward(now)
 
         @pl.when(jnp.logical_and(now >= plane, now < plane + chunks))
@@ -401,8 +394,7 @@
     lax.fori_loop(0, chunks + planes - 1, step, 0)
 
     def arrive(chunk, carry):
-        for peer in range(1, peers):
-            back_arrival(chunk, peer).wait_recv()
+        all_blocks(returned, chunk, back_recv)
         return carry
 
     span = field.shape[1]
@@ -422,9 +414,8 @@
             out[0, :, cols] = value if half == 0 else out[0, :, cols] + value
 
     def drain(chunk, carry):
-        for peer in range(1, peers):
-            go_copy(chunk, peer).wait_send()
-            back_copy(chunk, peer).wait_send()
+        all_blocks(send_box, chunk, go_send)
+        all_blocks(returned, chunk, back_send)
 
         @pl.when(plane < planes - 1)
         def _():
@@ -485,9 +476,9 @@
             pltpu.VMEM((chunks,) + wide, f32),
             pltpu.VMEM((chunks, levels, outer, rows, LANES), f32),
             pltpu.VMEM((chunks, peers, blocks, rows, LANES), f32),
-            dma((chunks, peers)), dma((chunks, peers)),
+            dma((chunks,)), dma((chunks,)),
             dma((chunks,)), dma((chunks,)), dma((chunks,)), dma((chunks,)),
-            dma((chunks, peers)), dma((chunks, peers)),
+            dma((chunks,)), dma((chunks,)),
         ],
         compiler_params=pltpu.CompilerParams(
             collective_id=0, has_side_effects=True, vmem_limit_bytes=56 * 1024 * 1024),

time: 68.7 us -> 66.6 us (0.969)
  Pallas kernels: 65.3 us -> 63.3 us
    pallas_call x1, Pallas kernels: 65.3 us -> 63.3 us  [local(): pl.pallas_call(functools.partial(kernel, cfg), out_shape=jax.ShapeDtypeSt...]
where the time goes in v2:
time: 66.6 us; the launch traced here: 66.4 us
  Pallas kernels  63.3 us (95%)
  local copies, waits for them, and re-layouts  3.16 us (5%)
    pallas_call x1, Pallas kernels, local(): pl.pallas_call(functools.partial(kernel, cfg), out_shape=jax.ShapeDtypeSt...  63.3 us
    unnamed x1, local copies, waits for them, and re-layouts  3.16 us

profile of v2, /device:TPU:0, one launch (start us, length us, event | category | flops | bytes accessed | tf_op | source)
XLA Modules:
  0.0 66.4 jit_solution(12082552145543723730)
XLA Ops:
  0.0 63.3 %shard_map.127 = f32[1,512,1024]{2,1,0:T(8,128)} custom-call(f32[8]{0:T(128)} %coupling.1, f32[8]{0:T(128)} %spacing.1, f32[1,512,1024]{2,1,0:T(8,128)} %field.1, bf16[512,512]{1,0:T(8,128)(2,1)} %constant.20.clone.span_high, bf16[512,512]{1,0:T(8,128)(2,1)} %constant.21.clone.span_low, bf16[2,256,256]{2,1,0:T(8,128)(2,1)} %constant.22.clone.fwd_high, ...), custom_call_target="tpu_custom_call" | custom-call | flops 8000000000 | bytes 8388608 | tf_op jit(solution)/shard_map/pallas_call | solution.py:458
  63.3 3.2 %copy.15 = f32[1,512,1024]{2,1,0:T(8,128)} copy(f32[1,512,1024]{2,1,0:T(8,128)} %shard_map.127) | data formatting | bytes 4194304

commit v3 on v2

--- a/solution.py
+++ b/solution.py
@@ -363,12 +363,16 @@
             return carry
 
         lax.fori_loop(0, levels * tiles, tile_step, 0)
+        returned[chunk, me] = solved[chunk, row, pl.ds(gx * blocks, blocks)]
+
+    def send_back(chunk, carry):
         for step in range(1, peers):
             back_copy(chunk, step).start()
-        returned[chunk, me] = solved[chunk, row, pl.ds(gx * blocks, blocks)]
+        return carry
 
     lag_down = planes - 1 - plane
     lag = jnp.maximum(plane, lag_down)
+    hold = jnp.maximum(lag, chunks - 2)
 
     def step(now, carry):
         @pl.when(now < chunks)
@@ -388,6 +392,10 @@
         @pl.when(jnp.logical_and(now >= lag, now < lag + chunks))
         def _():
             finish(now - lag)
+
+            @pl.when(now >= hold)
+            def _():
+                lax.fori_loop(jnp.where(now == hold, 0, now - lag), now - lag + 1, send_back, 0)
 
         return carry
 

time: 66.6 us -> 67.5 us (1.014)
  Pallas kernels: 63.3 us -> 64.1 us
    pallas_call x1, Pallas kernels: 63.3 us -> 64.1 us  [local(): pl.pallas_call(functools.partial(kernel, cfg), out_shape=jax.ShapeDtypeSt...]
where the time goes in v3:
time: 67.5 us; the launch traced here: 67.2 us
  Pallas kernels  64.1 us (95%)
  local copies, waits for them, and re-layouts  3.16 us (5%)
    pallas_call x1, Pallas kernels, local(): pl.pallas_call(functools.partial(kernel, cfg), out_shape=jax.ShapeDtypeSt...  64.1 us
    unnamed x1, local copies, waits for them, and re-layouts  3.16 us

profile of v3, /device:TPU:0, one launch (start us, length us, event | category | flops | bytes accessed | tf_op | source)
XLA Modules:
  0.0 67.2 jit_solution(4800114093994753516)
XLA Ops:
  0.0 64.1 %shard_map.127 = f32[1,512,1024]{2,1,0:T(8,128)} custom-call(f32[8]{0:T(128)} %coupling.1, f32[8]{0:T(128)} %spacing.1, f32[1,512,1024]{2,1,0:T(8,128)} %field.1, bf16[512,512]{1,0:T(8,128)(2,1)} %constant.20.clone.span_high, bf16[512,512]{1,0:T(8,128)(2,1)} %constant.21.clone.span_low, bf16[2,256,256]{2,1,0:T(8,128)(2,1)} %constant.22.clone.fwd_high, ...), custom_call_target="tpu_custom_call" | custom-call | flops 8000000000 | bytes 8388608 | tf_op jit(solution)/shard_map/pallas_call | solution.py:466
  64.1 3.2 %copy.15 = f32[1,512,1024]{2,1,0:T(8,128)} copy(f32[1,512,1024]{2,1,0:T(8,128)} %shard_map.127) | data formatting | bytes 4194304

commit v4 on v2

--- a/solution.py
+++ b/solution.py
@@ -42,12 +42,11 @@
     forward_high, forward_low = split_table(forward)
     inverse_high, inverse_low = split_table(inverse)
     turn_cos, turn_sin = cos_sin(np.arange(slots)[:, None] * lane[None, :], stream)
-    wave = np.arange(slots)[:, None] + outer * np.concatenate([lane, lane])[None, :]
-    wave[0, LANES:] += slots
+    wave = np.arange(slots + 1)[:, None] + outer * lane[None, :]
     eigen_stream = 2.0 - 2.0 * cos_sin(wave, stream)[0]
-    eigen_stream = np.ascontiguousarray(np.broadcast_to(eigen_stream[:, None, :], (slots, rows, 2 * LANES)))
+    eigen_stream = np.ascontiguousarray(np.broadcast_to(eigen_stream[:, None, :], (slots + 1, rows, LANES)))
     eigen_span = 2.0 - 2.0 * cos_sin(ks, span)[0]
-    eigen_span = np.broadcast_to(eigen_span[:, None], (span, 2 * LANES)).reshape(span // rows, rows, 2 * LANES)
+    eigen_span = np.broadcast_to(eigen_span[:, None], (span, LANES)).reshape(span // rows, rows, LANES)
     return (
         span_high, span_low, forward_high, forward_low, inverse_high, inverse_low,
         turn_cos.astype(np.float32), turn_sin.astype(np.float32),
@@ -124,7 +123,7 @@
     reduced, edge_down, from_below, from_above, solved, returned,
     go_send, go_recv, up_send, up_recv, down_send, down_recv, back_send, back_recv,
 ):
-    gx_count, group, planes, chunks, rows, levels, batch = cfg
+    gx_count, group, planes, chunks, rows, levels, batch, back_groups = cfg
     peers = gx_count * group
     blocks = field.shape[2] // LANES
     outer = blocks * gx_count
@@ -153,25 +152,27 @@
     def _():
         pl.semaphore_signal(barrier, inc=1, device_id=(gx, gz + group), device_id_type=MESH)
 
-    def go_copy(chunk, step):
+    def go_copy(turn, step):
+        to_gx, to_row = partner(step)
+        here = pl.ds(turn * batch, batch)
+        return pltpu.make_async_remote_copy(
+            src_ref=send_box.at[here, to_gx * group + to_row],
+            dst_ref=columns.at[here, row, pl.ds(gx * blocks, blocks)],
+            send_sem=go_send.at[turn], recv_sem=go_recv.at[turn],
+            device_id=(to_gx, plane * group + to_row), device_id_type=MESH)
+
+    def back_copy(index, step):
+        begin, count = back_groups[index]
         to_gx, to_row = partner(step)
         return pltpu.make_async_remote_copy(
-            src_ref=send_box.at[chunk, to_gx * group + to_row],
-            dst_ref=columns.at[chunk, row, pl.ds(gx * blocks, blocks)],
-            send_sem=go_send.at[chunk], recv_sem=go_recv.at[chunk],
+            src_ref=solved.at[begin:begin + count, to_row, pl.ds(to_gx * blocks, blocks)],
+            dst_ref=returned.at[begin:begin + count, me],
+            send_sem=back_send.at[index], recv_sem=back_recv.at[index],
             device_id=(to_gx, plane * group + to_row), device_id_type=MESH)
 
-    def all_blocks(box, chunk, sem):
-        blocks_here = box.at[chunk, pl.ds(0, peers - 1)]
-        pltpu.make_async_copy(blocks_here, blocks_here, sem.at[chunk]).wait()
-
-    def back_copy(chunk, step):
-        to_gx, to_row = partner(step)
-        return pltpu.make_async_remote_copy(
-            src_ref=solved.at[chunk, to_row, pl.ds(to_gx * blocks, blocks)],
-            dst_ref=returned.at[chunk, me],
-            send_sem=back_send.at[chunk], recv_sem=back_recv.at[chunk],
-            device_id=(to_gx, plane * group + to_row), device_id_type=MESH)
+    def all_blocks(box, begin, count, sem):
+        blocks_here = box.at[pl.ds(begin, count), pl.ds(0, peers - 1)]
+        pltpu.make_async_copy(blocks_here, blocks_here, sem).wait()
 
     def up_copy(chunk):
         return pltpu.make_async_remote_copy(
@@ -211,10 +212,10 @@
             expected = peers - 1 + jnp.where(plane > 0, 1, 0) + jnp.where(plane < planes - 1, 1, 0)
             pl.semaphore_wait(barrier, expected)
 
+        for step in range(1, peers):
+            go_copy(turn, step).start()
         for index in range(batch):
             chunk = turn * batch + index
-            for step in range(1, peers):
-                go_copy(chunk, step).start()
             columns[chunk, row, pl.ds(gx * blocks, blocks)] = send_box[chunk, me]
         return carry
 
@@ -224,9 +225,19 @@
     parts = slots // part_slots
 
     def coefficients(chunk):
-        def part_step(part, carry):
-            take = pl.ds(part * part_slots, part_slots)
-            lam = eig_span[chunk * peers + me][None] + eig_stream[take]
+        def store(target, begin, value):
+            count = value.shape[0]
+            low, high = (1 if begin == 0 else 0), (count - 1 if begin + count == slots + 1 else count)
+            if low:
+                target[0, :, :LANES] = value[0]
+            if high < count:
+                target[0, :, LANES:] = value[high]
+            target[begin + low:begin + high, :, :LANES] = value[low:high]
+            target[begin + low:begin + high, :, LANES:] = value[low:high]
+
+        middle_unit = slots // 2 + 1
+        for begin, end in ((0, middle_unit), (middle_unit, slots + 1)):
+            lam = eig_span[chunk * peers + me][None] + eig_stream[begin:end]
 
             def diagonal(level):
                 return lam * spacing[level] + (below(level) + above(level))
@@ -245,19 +256,16 @@
             low = lax.fori_loop(0, first, from_ground, start)
             for own in range(levels):
                 after = from_ground(first + own, low)
-                pivots_low[chunk, own, take] = low[0] * inverse_of(after[0])
+                store(pivots_low.at[chunk, own], begin, low[0] * inverse_of(after[0]))
                 low = after
             top = lax.fori_loop(0, level_count - first - levels, from_top, start)
             edge = above(first + levels - 1)
             both = low[0] * top[0]
-            middle[chunk, take] = both * inverse_of(both - (edge * edge) * (low[1] * top[1]))
+            store(middle.at[chunk], begin, both * inverse_of(both - (edge * edge) * (low[1] * top[1])))
             for own in reversed(range(levels)):
                 after = from_top(level_count - 1 - first - own, top)
-                pivots_high[chunk, own, take] = top[0] * inverse_of(after[0])
+                store(pivots_high.at[chunk, own], begin, top[0] * inverse_of(after[0]))
                 top = after
-            return carry
-
-        lax.fori_loop(0, parts, part_step, 0)
 
     tiles = rows // 8
 
@@ -363,9 +371,12 @@
             return carry
 
         lax.fori_loop(0, levels * tiles, tile_step, 0)
-        for step in range(1, peers):
-            back_copy(chunk, step).start()
         returned[chunk, me] = solved[chunk, row, pl.ds(gx * blocks, blocks)]
+        for index, (begin, count) in enumerate(back_groups):
+            @pl.when(chunk == begin + count - 1)
+            def _():
+                for step in range(1, peers):
+                    back_copy(index, step).start()
 
     lag_down = planes - 1 - plane
     lag = jnp.maximum(plane, lag_down)
@@ -374,7 +385,11 @@
         @pl.when(now < chunks)
         def _():
             coefficients(now)
-            all_blocks(send_box, now, go_recv)
+
+            @pl.when(now % batch == 0)
+            def _():
+                all_blocks(send_box, now, batch, go_recv.at[now // batch])
+
             stream_forward(now)
 
         @pl.when(jnp.logical_and(now >= plane, now < plane + chunks))
@@ -392,17 +407,15 @@
         return carry
 
     lax.fori_loop(0, chunks + planes - 1, step, 0)
-
-    def arrive(chunk, carry):
-        all_blocks(returned, chunk, back_recv)
-        return carry
 
     span = field.shape[1]
     width = min(2, blocks)
     halves = 2 if chunks % 2 == 0 else 1
     depth = span // halves
     for half in range(halves):
-        lax.fori_loop(half * (chunks // halves), (half + 1) * (chunks // halves), arrive, 0)
+        for index, (begin, count) in enumerate(back_groups):
+            if half * (chunks // halves) <= begin < (half + 1) * (chunks // halves):
+                all_blocks(returned, begin, count, back_recv.at[index])
         near = slice(half * depth, (half + 1) * depth)
         here = slice(half * (chunks // halves), (half + 1) * (chunks // halves))
         left = (span_high[:, near], span_low[:, near])
@@ -414,9 +427,6 @@
             out[0, :, cols] = value if half == 0 else out[0, :, cols] + value
 
     def drain(chunk, carry):
-        all_blocks(send_box, chunk, go_send)
-        all_blocks(returned, chunk, back_send)
-
         @pl.when(plane < planes - 1)
         def _():
             up_copy(chunk).wait_send()
@@ -428,6 +438,10 @@
         return carry
 
     lax.fori_loop(0, chunks, drain, 0)
+    for turn in range(chunks // batch):
+        all_blocks(send_box, turn * batch, batch, go_send.at[turn])
+    for index, (begin, count) in enumerate(back_groups):
+        all_blocks(returned, begin, count, back_send.at[index])
 
 
 def local(mesh_shape, source_field, coupling, spacing):
@@ -445,6 +459,8 @@
         chunks //= 2
     rows = share // chunks
     batch = 2 if chunks % 2 == 0 and peers * rows < 128 else 1
+    paired = max(0, chunks - 2) // 2 * 2
+    back_groups = [(begin, 2) for begin in range(0, paired, 2)] + [(begin, 1) for begin in range(paired, chunks)]
     blocks = part // LANES
     outer = stream // LANES
     slots = outer // 2
@@ -454,7 +470,7 @@
     dma = pltpu.SemaphoreType.DMA
     vmem = pl.BlockSpec(memory_space=pltpu.VMEM)
     smem = pl.BlockSpec(memory_space=pltpu.SMEM)
-    cfg = (gx_count, group, planes, chunks, rows, levels, batch)
+    cfg = (gx_count, group, planes, chunks, rows, levels, batch, back_groups)
     return pl.pallas_call(
         functools.partial(kernel, cfg),
         out_shape=jax.ShapeDtypeStruct(source_field.shape, f32),
@@ -476,9 +492,9 @@
             pltpu.VMEM((chunks,) + wide, f32),
             pltpu.VMEM((chunks, levels, outer, rows, LANES), f32),
             pltpu.VMEM((chunks, peers, blocks, rows, LANES), f32),
-            dma((chunks,)), dma((chunks,)),
+            dma((chunks // batch,)), dma((chunks // batch,)),
             dma((chunks,)), dma((chunks,)), dma((chunks,)), dma((chunks,)),
-            dma((chunks,)), dma((chunks,)),
+            dma((len(back_groups),)), dma((len(back_groups),)),
         ],
         compiler_params=pltpu.CompilerParams(
             collective_id=0, has_side_effects=True, vmem_limit_bytes=56 * 1024 * 1024),

time: 66.6 us -> 67.2 us (level)
  no operation moved by 1% of the time
where the time goes in v4:
time: 67.2 us; the launch traced here: 67 us
  Pallas kernels  63.8 us (95%)
  local copies, waits for them, and re-layouts  3.16 us (5%)
    pallas_call x1, Pallas kernels, local(): pl.pallas_call(functools.partial(kernel, cfg), out_shape=jax.ShapeDtypeSt...  63.8 us
    unnamed x1, local copies, waits for them, and re-layouts  3.16 us

profile of v4, /device:TPU:0, one launch (start us, length us, event | category | flops | bytes accessed | tf_op | source)
XLA Modules:
  0.0 67.0 jit_solution(16281443517032195804)
XLA Ops:
  0.0 63.8 %shard_map.127 = f32[1,512,1024]{2,1,0:T(8,128)} custom-call(f32[8]{0:T(128)} %coupling.1, f32[8]{0:T(128)} %spacing.1, f32[1,512,1024]{2,1,0:T(8,128)} %field.1, bf16[512,512]{1,0:T(8,128)(2,1)} %constant.20.clone.span_high, bf16[512,512]{1,0:T(8,128)(2,1)} %constant.21.clone.span_low, bf16[2,256,256]{2,1,0:T(8,128)(2,1)} %constant.22.clone.fwd_high, ...), custom_call_target="tpu_custom_call" | custom-call | flops 8000000000 | bytes 8388608 | tf_op jit(solution)/shard_map/pallas_call | solution.py:474
  63.8 3.2 %copy.15 = f32[1,512,1024]{2,1,0:T(8,128)} copy(f32[1,512,1024]{2,1,0:T(8,128)} %shard_map.127) | data formatting | bytes 4194304

commit v5 on v4

--- a/solution.py
+++ b/solution.py
@@ -118,10 +118,10 @@
 
 def kernel(
     cfg, coupling, spacing, field, span_high, span_low, fwd_high, fwd_low, inv_high, inv_low,
-    turn_cos, turn_sin, eig_stream, eig_span, out,
+    turn_cos, turn_sin, eig_stream, eig_span, returned,
     field_high, field_low, send_box, columns, staging, spectrum, pivots_low, pivots_high, middle,
-    reduced, edge_down, from_below, from_above, solved, returned,
-    go_send, go_recv, up_send, up_recv, down_send, down_recv, back_send, back_recv,
+    reduced, edge_down, from_below, from_above, solved,
+    go_send, go_recv, up_send, up_recv, down_send, down_recv, back_send, back_recv, own_sem,
 ):
     gx_count, group, planes, chunks, rows, levels, batch, back_groups = cfg
     peers = gx_count * group
@@ -169,6 +169,10 @@
             dst_ref=returned.at[begin:begin + count, me],
             send_sem=back_send.at[index], recv_sem=back_recv.at[index],
             device_id=(to_gx, plane * group + to_row), device_id_type=MESH)
+
+    def own_copy(chunk):
+        return pltpu.make_async_copy(
+            solved.at[chunk, row, pl.ds(gx * blocks, blocks)], returned.at[chunk, me], own_sem.at[chunk])
 
     def all_blocks(box, begin, count, sem):
         blocks_here = box.at[pl.ds(begin, count), pl.ds(0, peers - 1)]
@@ -371,7 +375,7 @@
             return carry
 
         lax.fori_loop(0, levels * tiles, tile_step, 0)
-        returned[chunk, me] = solved[chunk, row, pl.ds(gx * blocks, blocks)]
+        own_copy(chunk).start()
         for index, (begin, count) in enumerate(back_groups):
             @pl.when(chunk == begin + count - 1)
             def _():
@@ -408,25 +412,12 @@
 
     lax.fori_loop(0, chunks + planes - 1, step, 0)
 
-    span = field.shape[1]
-    width = min(2, blocks)
-    halves = 2 if chunks % 2 == 0 else 1
-    depth = span // halves
-    for half in range(halves):
-        for index, (begin, count) in enumerate(back_groups):
-            if half * (chunks // halves) <= begin < (half + 1) * (chunks // halves):
-                all_blocks(returned, begin, count, back_recv.at[index])
-        near = slice(half * depth, (half + 1) * depth)
-        here = slice(half * (chunks // halves), (half + 1) * (chunks // halves))
-        left = (span_high[:, near], span_low[:, near])
-        for block in range(0, blocks, width):
-            pieces = [returned[here, :, block + part].reshape(depth, LANES) for part in range(width)]
-            right = split_value(jnp.concatenate(pieces, axis=1) if width > 1 else pieces[0])
-            value = dot3(left, right)
-            cols = slice(block * LANES, (block + width) * LANES)
-            out[0, :, cols] = value if half == 0 else out[0, :, cols] + value
+    for index, (begin, count) in enumerate(back_groups):
+        all_blocks(send_box, begin, count, back_recv.at[index])
 
     def drain(chunk, carry):
+        own_copy(chunk).wait()
+
         @pl.when(plane < planes - 1)
         def _():
             up_copy(chunk).wait_send()
@@ -441,7 +432,14 @@
     for turn in range(chunks // batch):
         all_blocks(send_box, turn * batch, batch, go_send.at[turn])
     for index, (begin, count) in enumerate(back_groups):
-        all_blocks(returned, begin, count, back_send.at[index])
+        all_blocks(send_box, begin, count, back_send.at[index])
+
+
+def last_product(returned, span_high, span_low, out):
+    span, width = out.shape[1], out.shape[2] // LANES
+    pieces = [returned[:, :, part].reshape(span, LANES) for part in range(width)]
+    right = split_value(jnp.concatenate(pieces, axis=1) if width > 1 else pieces[0])
+    out[0] = dot3((span_high[...], span_low[...]), right)
 
 
 def local(mesh_shape, source_field, coupling, spacing):
@@ -471,11 +469,13 @@
     vmem = pl.BlockSpec(memory_space=pltpu.VMEM)
     smem = pl.BlockSpec(memory_space=pltpu.SMEM)
     cfg = (gx_count, group, planes, chunks, rows, levels, batch, back_groups)
-    return pl.pallas_call(
+    box = (chunks, peers, blocks, rows, LANES)
+    tables = [jnp.asarray(table) for table in tables]
+    returned = pl.pallas_call(
         functools.partial(kernel, cfg),
-        out_shape=jax.ShapeDtypeStruct(source_field.shape, f32),
+        out_shape=jax.ShapeDtypeStruct(box, f32),
         in_specs=[smem, smem] + [vmem] * 11,
-        out_specs=vmem,
+        out_specs=pl.BlockSpec(memory_space=pl.ANY),
         scratch_shapes=[
             pltpu.VMEM((span, part), jnp.bfloat16),
             pltpu.VMEM((span, part), jnp.bfloat16),
@@ -491,15 +491,28 @@
             pltpu.VMEM((chunks,) + wide, f32),
             pltpu.VMEM((chunks,) + wide, f32),
             pltpu.VMEM((chunks, levels, outer, rows, LANES), f32),
-            pltpu.VMEM((chunks, peers, blocks, rows, LANES), f32),
             dma((chunks // batch,)), dma((chunks // batch,)),
             dma((chunks,)), dma((chunks,)), dma((chunks,)), dma((chunks,)),
-            dma((len(back_groups),)), dma((len(back_groups),)),
+            dma((len(back_groups),)), dma((len(back_groups),)), dma((chunks,)),
         ],
         compiler_params=pltpu.CompilerParams(
             collective_id=0, has_side_effects=True, vmem_limit_bytes=56 * 1024 * 1024),
         cost_estimate=pl.CostEstimate(flops=8 * 10**9, bytes_accessed=8 * 2**20, transcendentals=0),
-    )(coupling, spacing, source_field, *(jnp.asarray(table) for table in tables))
+    )(coupling, spacing, source_field, *tables)
+    width = min(2, blocks)
+    return pl.pallas_call(
+        last_product,
+        grid=(blocks // width,),
+        out_shape=jax.ShapeDtypeStruct(source_field.shape, f32),
+        in_specs=[
+            pl.BlockSpec((chunks, peers, width, rows, LANES), lambda index: (0, 0, index, 0, 0)),
+            pl.BlockSpec((span, span), lambda index: (0, 0)),
+            pl.BlockSpec((span, span), lambda index: (0, 0)),
+        ],
+        out_specs=pl.BlockSpec((1, span, width * LANES), lambda index: (0, 0, index)),
+        compiler_params=pltpu.CompilerParams(vmem_limit_bytes=32 * 1024 * 1024),
+        cost_estimate=pl.CostEstimate(flops=2 * 10**9, bytes_accessed=5 * 2**20, transcendentals=0),
+    )(returned, tables[0], tables[1])
 
 
 def solution(mesh):

time: 67.2 us -> 67.3 us (level)
  local copies, waits for them, and re-layouts: 3.16 us -> 1.59 us
  Pallas kernels: 63.8 us -> 65.3 us
    pallas_call x0 -> x1, Pallas kernels: none -> 3.47 us  [local(): pl.pallas_call(last_product, grid=(blocks // width,), out_shape=jax.Shape...]
    pallas_call x1, Pallas kernels: 63.8 us -> 61.8 us  [local(): pl.pallas_call(functools.partial(kernel, cfg), out_shape=jax.ShapeDtypeSt...]
    unnamed x1 -> x6, local copies, waits for them, and re-layouts: 3.16 us -> 1.59 us
where the time goes in v5:
time: 67.3 us; the launch traced here: 66.9 us
  Pallas kernels  65.3 us (97%)
  local copies, waits for them, and re-layouts  1.59 us (2%)
    pallas_call x1, Pallas kernels, local(): pl.pallas_call(functools.partial(kernel, cfg), out_shape=jax.ShapeDtypeSt...  61.8 us
    pallas_call x1, Pallas kernels, local(): pl.pallas_call(last_product, grid=(blocks // width,), out_shape=jax.Shape...  3.47 us
    unnamed x6, local copies, waits for them, and re-layouts  1.59 us

profile of v5, /device:TPU:0, one launch (start us, length us, event | category | flops | bytes accessed | tf_op | source)
XLA Modules:
  0.0 66.9 jit_solution(15263605299808168198)
XLA Ops:
  0.0 0.0 copy-start
  0.0 0.0 copy-start.1
  0.0 61.8 %shard_map.127.returned = f32[8,8,8,8,128]{4,3,2,1,0:T(8,128)} custom-call(f32[8]{0:T(128)} %coupling.1, f32[8]{0:T(128)} %spacing.1, f32[1,512,1024]{2,1,0:T(8,128)} %field.1, bf16[512,512]{1,0:T(8,128)(2,1)} %constant.20.clone.span_high, bf16[512,512]{1,0:T(8,128)(2,1)} %constant.21.clone.span_low, bf16[2,256,256]{2,1,0:T(8,128)(2,1)} %constant.22.clone.fwd_high, ...), custom_call_target="tpu_custom_call" | custom-call | flops 8000000000 | bytes 8388608 | tf_op jit(solution)/shard_map/pallas_call | solution.py:474
  61.8 0.0 copy-done
  61.9 0.0 copy-done.1
  61.9 0.0 copy-start.2
  61.9 1.6 %copy-done.2 = f32[8,8,8,8,128]{4,3,2,1,0:T(8,128)S(1)} copy-done((f32[8,8,8,8,128]{4,3,2,1,0:T(8,128)S(1)}, f32[8,8,8,8,128]{4,3,2,1,0:T(8,128)}, u32[]{:S(2)}) %copy-start.2) | copy-done | bytes 2097176
  63.5 3.5 %shard_map.128 = f32[1,512,1024]{2,1,0:T(8,128)} custom-call(f32[8,8,8,8,128]{4,3,2,1,0:T(8,128)S(1)} %copy-done.2, bf16[512,512]{1,0:T(8,128)(2,1)S(1)} %copy-done.1, bf16[512,512]{1,0:T(8,128)(2,1)S(1)} %copy-done), custom_call_target="tpu_custom_call" | custom-call | flops 2000000000 | bytes 5242880 | tf_op jit(solution)/shard_map/pallas_call | solution.py:503
Async XLA Ops:
  0.0 61.8 %copy-start = (bf16[512,512]{1,0:T(8,128)(2,1)S(1)}, bf16[512,512]{1,0:T(8,128)(2,1)}, u32[]{:S(2)}) copy-start(bf16[512,512]{1,0:T(8,128)(2,1)} %constant.21.clone.span_low) | copy-start | bytes 1572868
  0.0 61.9 %copy-start.1 = (bf16[512,512]{1,0:T(8,128)(2,1)S(1)}, bf16[512,512]{1,0:T(8,128)(2,1)}, u32[]{:S(2)}) copy-start(bf16[512,512]{1,0:T(8,128)(2,1)} %constant.20.clone.span_high) | copy-start | bytes 1572868
  61.9 1.6 %copy-start.2 = (f32[8,8,8,8,128]{4,3,2,1,0:T(8,128)S(1)}, f32[8,8,8,8,128]{4,3,2,1,0:T(8,128)}, u32[]{:S(2)}) copy-start(f32[8,8,8,8,128]{4,3,2,1,0:T(8,128)} %shard_map.127.returned) | copy-start | bytes 6291460

commit v6 on v5

--- a/solution.py
+++ b/solution.py
@@ -178,16 +178,21 @@
         blocks_here = box.at[pl.ds(begin, count), pl.ds(0, peers - 1)]
         pltpu.make_async_copy(blocks_here, blocks_here, sem).wait()
 
-    def up_copy(chunk):
+    part_slots = min(max(1, 32 // rows), slots)
+    parts = slots // part_slots
+
+    def up_copy(chunk, part):
+        take = pl.ds(part * part_slots, part_slots)
         return pltpu.make_async_remote_copy(
-            src_ref=reduced.at[chunk, levels - 1], dst_ref=from_below.at[chunk],
-            send_sem=up_send.at[chunk], recv_sem=up_recv.at[chunk],
+            src_ref=reduced.at[chunk, levels - 1, take], dst_ref=from_below.at[chunk, take],
+            send_sem=up_send.at[chunk, part], recv_sem=up_recv.at[chunk, part],
             device_id=(gx, (gz + group) % (planes * group)), device_id_type=MESH)
 
-    def down_copy(chunk):
+    def down_copy(chunk, part):
+        take = pl.ds(part * part_slots, part_slots)
         return pltpu.make_async_remote_copy(
-            src_ref=edge_down.at[chunk], dst_ref=from_above.at[chunk],
-            send_sem=down_send.at[chunk], recv_sem=down_recv.at[chunk],
+            src_ref=edge_down.at[chunk, take], dst_ref=from_above.at[chunk, take],
+            send_sem=down_send.at[chunk, part], recv_sem=down_recv.at[chunk, part],
             device_id=(gx, (gz + planes * group - group) % (planes * group)), device_id_type=MESH)
 
     def below(level):
@@ -224,9 +229,6 @@
         return carry
 
     lax.fori_loop(0, chunks // batch, span_step, 0)
-
-    part_slots = min(max(1, 64 // rows), slots)
-    parts = slots // part_slots
 
     def coefficients(chunk):
         def store(target, begin, value):
@@ -296,51 +298,45 @@
         spectrum[chunk, 1:] = regular.reshape(slots - 1, levels, rows, 2 * LANES)
 
     def sweep_up(chunk):
-        @pl.when(plane > 0)
-        def _():
-            up_copy(chunk).wait_recv()
-
         @pl.when(plane == 0)
         def _():
             from_below[chunk] = jnp.zeros(from_below.shape[1:], jnp.float32)
 
-        def part_step(part, carry):
+        for part in range(parts):
+            @pl.when(plane > 0)
+            def _():
+                up_copy(chunk, part).wait_recv()
+
             take = pl.ds(part * part_slots, part_slots)
             value = from_below[chunk, take]
             for own in range(levels):
                 level = first + own
                 value = (spacing[level] * spectrum[chunk, take, own] + below(level) * value) * pivots_low[chunk, own, take]
                 reduced[chunk, own, take] = value
-            return carry
-
-        lax.fori_loop(0, parts, part_step, 0)
-
-        @pl.when(plane < planes - 1)
-        def _():
-            up_copy(chunk).start()
+
+            @pl.when(plane < planes - 1)
+            def _():
+                up_copy(chunk, part).start()
 
     def sweep_down(chunk):
-        @pl.when(plane < planes - 1)
-        def _():
-            down_copy(chunk).wait_recv()
-
         @pl.when(plane == planes - 1)
         def _():
             from_above[chunk] = jnp.zeros(from_above.shape[1:], jnp.float32)
 
-        @pl.when(plane > 0)
-        def _():
-            def part_step(part, carry):
+        for part in range(parts):
+            @pl.when(plane < planes - 1)
+            def _():
+                down_copy(chunk, part).wait_recv()
+
+            @pl.when(plane > 0)
+            def _():
                 take = pl.ds(part * part_slots, part_slots)
                 value = from_above[chunk, take]
                 for own in reversed(range(levels)):
                     level = first + own
                     value = (spacing[level] * spectrum[chunk, take, own] + above(level) * value) * pivots_high[chunk, own, take]
                 edge_down[chunk, take] = value
-                return carry
-
-            lax.fori_loop(0, parts, part_step, 0)
-            down_copy(chunk).start()
+                down_copy(chunk, part).start()
 
     def finish(chunk):
         def part_step(part, carry):
@@ -418,13 +414,14 @@
     def drain(chunk, carry):
         own_copy(chunk).wait()
 
-        @pl.when(plane < planes - 1)
-        def _():
-            up_copy(chunk).wait_send()
-
-        @pl.when(plane > 0)
-        def _():
-            down_copy(chunk).wait_send()
+        for part in range(parts):
+            @pl.when(plane < planes - 1)
+            def _():
+                up_copy(chunk, part).wait_send()
+
+            @pl.when(plane > 0)
+            def _():
+                down_copy(chunk, part).wait_send()
 
         return carry
 
@@ -465,6 +462,7 @@
     tables = make_tables(span, stream, rows)
     f32 = jnp.float32
     wide = (slots, rows, 2 * LANES)
+    parts = slots // min(max(1, 32 // rows), slots)
     dma = pltpu.SemaphoreType.DMA
     vmem = pl.BlockSpec(memory_space=pltpu.VMEM)
     smem = pl.BlockSpec(memory_space=pltpu.SMEM)
@@ -492,7 +490,7 @@
             pltpu.VMEM((chunks,) + wide, f32),
             pltpu.VMEM((chunks, levels, outer, rows, LANES), f32),
             dma((chunks // batch,)), dma((chunks // batch,)),
-            dma((chunks,)), dma((chunks,)), dma((chunks,)), dma((chunks,)),
+            *[dma((chunks, parts)) for _ in range(4)],
             dma((len(back_groups),)), dma((len(back_groups),)), dma((chunks,)),
         ],
         compiler_params=pltpu.CompilerParams(
@@ -510,7 +508,7 @@
             pl.BlockSpec((span, span), lambda index: (0, 0)),
         ],
         out_specs=pl.BlockSpec((1, span, width * LANES), lambda index: (0, 0, index)),
-        compiler_params=pltpu.CompilerParams(vmem_limit_bytes=32 * 1024 * 1024),
+        compiler_params=pltpu.CompilerParams(vmem_limit_bytes=56 * 1024 * 1024),
         cost_estimate=pl.CostEstimate(flops=2 * 10**9, bytes_accessed=5 * 2**20, transcendentals=0),
     )(returned, tables[0], tables[1])
 

time: 67.3 us -> 63.2 us (0.939)
  Pallas kernels: 65.3 us -> 62.9 us
  local copies, waits for them, and re-layouts: 1.59 us -> 0 us
    pallas_call x1, Pallas kernels: 61.8 us -> 57.7 us  [local(): pl.pallas_call(functools.partial(kernel, cfg), out_shape=jax.ShapeDtypeSt...]
    pallas_call x1, Pallas kernels: 3.47 us -> 5.22 us  [local(): pl.pallas_call(last_product, grid=(blocks // width,), out_shape=jax.Shape...]
    unnamed x6 -> x0, local copies, waits for them, and re-layouts: 1.59 us -> none
where the time goes in v6:
time: 63.2 us; the launch traced here: 62.9 us
  Pallas kernels  62.9 us (100%)
    pallas_call x1, Pallas kernels, local(): pl.pallas_call(functools.partial(kernel, cfg), out_shape=jax.ShapeDtypeSt...  57.7 us
    pallas_call x1, Pallas kernels, local(): pl.pallas_call(last_product, grid=(blocks // width,), out_shape=jax.Shape...  5.22 us

profile of v6, /device:TPU:0, one launch (start us, length us, event | category | flops | bytes accessed | tf_op | source)
XLA Modules:
  0.0 62.9 jit_solution(14959905848127914509)
XLA Ops:
  0.0 57.7 %shard_map.127.returned = f32[8,8,8,8,128]{4,3,2,1,0:T(8,128)} custom-call(f32[8]{0:T(128)} %coupling.1, f32[8]{0:T(128)} %spacing.1, f32[1,512,1024]{2,1,0:T(8,128)} %field.1, bf16[512,512]{1,0:T(8,128)(2,1)} %constant.20.clone.span_high, bf16[512,512]{1,0:T(8,128)(2,1)} %constant.21.clone.span_low, bf16[2,256,256]{2,1,0:T(8,128)(2,1)} %constant.22.clone.fwd_high, ...), custom_call_target="tpu_custom_call" | custom-call | flops 8000000000 | bytes 8388608 | tf_op jit(solution)/shard_map/pallas_call | solution.py:472
  57.7 5.2 %shard_map.128 = f32[1,512,1024]{2,1,0:T(8,128)} custom-call(f32[8,8,8,8,128]{4,3,2,1,0:T(8,128)} %shard_map.127.returned, bf16[512,512]{1,0:T(8,128)(2,1)} %constant.20.clone.span_high, bf16[512,512]{1,0:T(8,128)(2,1)} %constant.21.clone.span_low), custom_call_target="tpu_custom_call" | custom-call | flops 2000000000 | bytes 5242880 | tf_op jit(solution)/shard_map/pallas_call | solution.py:501

commit v7 on v6

--- a/solution.py
+++ b/solution.py
@@ -152,13 +152,12 @@
     def _():
         pl.semaphore_signal(barrier, inc=1, device_id=(gx, gz + group), device_id_type=MESH)
 
-    def go_copy(turn, step):
+    def go_copy(chunk, step):
         to_gx, to_row = partner(step)
-        here = pl.ds(turn * batch, batch)
         return pltpu.make_async_remote_copy(
-            src_ref=send_box.at[here, to_gx * group + to_row],
-            dst_ref=columns.at[here, row, pl.ds(gx * blocks, blocks)],
-            send_sem=go_send.at[turn], recv_sem=go_recv.at[turn],
+            src_ref=send_box.at[chunk, to_gx * group + to_row],
+            dst_ref=columns.at[chunk, row, pl.ds(gx * blocks, blocks)],
+            send_sem=go_send.at[chunk], recv_sem=go_recv.at[chunk],
             device_id=(to_gx, plane * group + to_row), device_id_type=MESH)
 
     def back_copy(index, step):
@@ -221,10 +220,10 @@
             expected = peers - 1 + jnp.where(plane > 0, 1, 0) + jnp.where(plane < planes - 1, 1, 0)
             pl.semaphore_wait(barrier, expected)
 
-        for step in range(1, peers):
-            go_copy(turn, step).start()
         for index in range(batch):
             chunk = turn * batch + index
+            for step in range(1, peers):
+                go_copy(chunk, step).start()
             columns[chunk, row, pl.ds(gx * blocks, blocks)] = send_box[chunk, me]
         return carry
 
@@ -385,11 +384,7 @@
         @pl.when(now < chunks)
         def _():
             coefficients(now)
-
-            @pl.when(now % batch == 0)
-            def _():
-                all_blocks(send_box, now, batch, go_recv.at[now // batch])
-
+            all_blocks(send_box, now, 1, go_recv.at[now])
             stream_forward(now)
 
         @pl.when(jnp.logical_and(now >= plane, now < plane + chunks))
@@ -426,8 +421,8 @@
         return carry
 
     lax.fori_loop(0, chunks, drain, 0)
-    for turn in range(chunks // batch):
-        all_blocks(send_box, turn * batch, batch, go_send.at[turn])
+    for chunk in range(chunks):
+        all_blocks(send_box, chunk, 1, go_send.at[chunk])
     for index, (begin, count) in enumerate(back_groups):
         all_blocks(send_box, begin, count, back_send.at[index])
 
@@ -454,8 +449,7 @@
         chunks //= 2
     rows = share // chunks
     batch = 2 if chunks % 2 == 0 and peers * rows < 128 else 1
-    paired = max(0, chunks - 2) // 2 * 2
-    back_groups = [(begin, 2) for begin in range(0, paired, 2)] + [(begin, 1) for begin in range(paired, chunks)]
+    back_groups = [(begin, 1) for begin in range(chunks)]
     blocks = part // LANES
     outer = stream // LANES
     slots = outer // 2
@@ -489,7 +483,7 @@
             pltpu.VMEM((chunks,) + wide, f32),
             pltpu.VMEM((chunks,) + wide, f32),
             pltpu.VMEM((chunks, levels, outer, rows, LANES), f32),
-            dma((chunks // batch,)), dma((chunks // batch,)),
+            dma((chunks,)), dma((chunks,)),
             *[dma((chunks, parts)) for _ in range(4)],
             dma((len(back_groups),)), dma((len(back_groups),)), dma((chunks,)),
         ],

time: 63.2 us -> 59.8 us (0.946)
  Pallas kernels: 62.9 us -> 59.6 us
    pallas_call x1, Pallas kernels: 57.7 us -> 54.4 us  [local(): pl.pallas_call(functools.partial(kernel, cfg), out_shape=jax.ShapeDtypeSt...]
where the time goes in v7:
time: 59.8 us; the launch traced here: 59.6 us
  Pallas kernels  59.6 us (100%)
    pallas_call x1, Pallas kernels, local(): pl.pallas_call(functools.partial(kernel, cfg), out_shape=jax.ShapeDtypeSt...  54.4 us
    pallas_call x1, Pallas kernels, local(): pl.pallas_call(last_product, grid=(blocks // width,), out_shape=jax.Shape...  5.22 us

profile of v7, /device:TPU:0, one launch (start us, length us, event | category | flops | bytes accessed | tf_op | source)
XLA Modules:
  0.0 59.6 jit_solution(9718327341909416592)
XLA Ops:
  0.0 54.4 %shard_map.127.returned = f32[8,8,8,8,128]{4,3,2,1,0:T(8,128)} custom-call(f32[8]{0:T(128)} %coupling.1, f32[8]{0:T(128)} %spacing.1, f32[1,512,1024]{2,1,0:T(8,128)} %field.1, bf16[512,512]{1,0:T(8,128)(2,1)} %constant.20.clone.span_high, bf16[512,512]{1,0:T(8,128)(2,1)} %constant.21.clone.span_low, bf16[2,256,256]{2,1,0:T(8,128)(2,1)} %constant.22.clone.fwd_high, ...), custom_call_target="tpu_custom_call" | custom-call | flops 8000000000 | bytes 8388608 | tf_op jit(solution)/shard_map/pallas_call | solution.py:466
  54.4 5.2 %shard_map.128 = f32[1,512,1024]{2,1,0:T(8,128)} custom-call(f32[8,8,8,8,128]{4,3,2,1,0:T(8,128)} %shard_map.127.returned, bf16[512,512]{1,0:T(8,128)(2,1)} %constant.20.clone.span_high, bf16[512,512]{1,0:T(8,128)(2,1)} %constant.21.clone.span_low), custom_call_target="tpu_custom_call" | custom-call | flops 2000000000 | bytes 5242880 | tf_op jit(solution)/shard_map/pallas_call | solution.py:495

commit v8 on v7

--- a/solution.py
+++ b/solution.py
@@ -222,7 +222,7 @@
 
         for index in range(batch):
             chunk = turn * batch + index
-            for step in range(1, peers):
+            for step in reversed(range(1, peers)):
                 go_copy(chunk, step).start()
             columns[chunk, row, pl.ds(gx * blocks, blocks)] = send_box[chunk, me]
         return carry
@@ -374,7 +374,7 @@
         for index, (begin, count) in enumerate(back_groups):
             @pl.when(chunk == begin + count - 1)
             def _():
-                for step in range(1, peers):
+                for step in reversed(range(1, peers)):
                     back_copy(index, step).start()
 
     lag_down = planes - 1 - plane

time: 59.8 us -> 60.5 us (1.012)
  Pallas kernels: 59.6 us -> 60.3 us
    pallas_call x1, Pallas kernels: 54.4 us -> 55.1 us  [local(): pl.pallas_call(functools.partial(kernel, cfg), out_shape=jax.ShapeDtypeSt...]
where the time goes in v8:
time: 60.5 us; the launch traced here: 60.3 us
  Pallas kernels  60.3 us (100%)
    pallas_call x1, Pallas kernels, local(): pl.pallas_call(functools.partial(kernel, cfg), out_shape=jax.ShapeDtypeSt...  55.1 us
    pallas_call x1, Pallas kernels, local(): pl.pallas_call(last_product, grid=(blocks // width,), out_shape=jax.Shape...  5.22 us

profile of v8, /device:TPU:0, one launch (start us, length us, event | category | flops | bytes accessed | tf_op | source)
XLA Modules:
  0.0 60.3 jit_solution(17832536273952033628)
XLA Ops:
  0.0 55.1 %shard_map.127.returned = f32[8,8,8,8,128]{4,3,2,1,0:T(8,128)} custom-call(f32[8]{0:T(128)} %coupling.1, f32[8]{0:T(128)} %spacing.1, f32[1,512,1024]{2,1,0:T(8,128)} %field.1, bf16[512,512]{1,0:T(8,128)(2,1)} %constant.20.clone.span_high, bf16[512,512]{1,0:T(8,128)(2,1)} %constant.21.clone.span_low, bf16[2,256,256]{2,1,0:T(8,128)(2,1)} %constant.22.clone.fwd_high, ...), custom_call_target="tpu_custom_call" | custom-call | flops 8000000000 | bytes 8388608 | tf_op jit(solution)/shard_map/pallas_call | solution.py:466
  55.1 5.2 %shard_map.128 = f32[1,512,1024]{2,1,0:T(8,128)} custom-call(f32[8,8,8,8,128]{4,3,2,1,0:T(8,128)} %shard_map.127.returned, bf16[512,512]{1,0:T(8,128)(2,1)} %constant.20.clone.span_high, bf16[512,512]{1,0:T(8,128)(2,1)} %constant.21.clone.span_low), custom_call_target="tpu_custom_call" | custom-call | flops 2000000000 | bytes 5242880 | tf_op jit(solution)/shard_map/pallas_call | solution.py:495

commit v9 on v7

--- a/solution.py
+++ b/solution.py
@@ -448,7 +448,7 @@
     while share % (8 * chunks):
         chunks //= 2
     rows = share // chunks
-    batch = 2 if chunks % 2 == 0 and peers * rows < 128 else 1
+    batch = 1
     back_groups = [(begin, 1) for begin in range(chunks)]
     blocks = part // LANES
     outer = stream // LANES

time: 59.8 us -> 61.3 us (1.025)
  Pallas kernels: 59.6 us -> 61 us
    pallas_call x1, Pallas kernels: 54.4 us -> 55.8 us  [local(): pl.pallas_call(functools.partial(kernel, cfg), out_shape=jax.ShapeDtypeSt...]
where the time goes in v9:
time: 61.3 us; the launch traced here: 61.1 us
  Pallas kernels  61 us (100%)
    pallas_call x1, Pallas kernels, local(): pl.pallas_call(functools.partial(kernel, cfg), out_shape=jax.ShapeDtypeSt...  55.8 us
    pallas_call x1, Pallas kernels, local(): pl.pallas_call(last_product, grid=(blocks // width,), out_shape=jax.Shape...  5.22 us

profile of v9, /device:TPU:0, one launch (start us, length us, event | category | flops | bytes accessed | tf_op | source)
XLA Modules:
  0.0 61.1 jit_solution(962830711845719371)
XLA Ops:
  0.0 55.8 %shard_map.127.returned = f32[8,8,8,8,128]{4,3,2,1,0:T(8,128)} custom-call(f32[8]{0:T(128)} %coupling.1, f32[8]{0:T(128)} %spacing.1, f32[1,512,1024]{2,1,0:T(8,128)} %field.1, bf16[512,512]{1,0:T(8,128)(2,1)} %constant.20.clone.span_high, bf16[512,512]{1,0:T(8,128)(2,1)} %constant.21.clone.span_low, bf16[2,256,256]{2,1,0:T(8,128)(2,1)} %constant.22.clone.fwd_high, ...), custom_call_target="tpu_custom_call" | custom-call | flops 8000000000 | bytes 8388608 | tf_op jit(solution)/shard_map/pallas_call | solution.py:466
  55.8 5.2 %shard_map.128 = f32[1,512,1024]{2,1,0:T(8,128)} custom-call(f32[8,8,8,8,128]{4,3,2,1,0:T(8,128)} %shard_map.127.returned, bf16[512,512]{1,0:T(8,128)(2,1)} %constant.20.clone.span_high, bf16[512,512]{1,0:T(8,128)(2,1)} %constant.21.clone.span_low), custom_call_target="tpu_custom_call" | custom-call | flops 2000000000 | bytes 5242880 | tf_op jit(solution)/shard_map/pallas_call | solution.py:495
